TPU v7x, 32 devices: a whole 2x2x4 slice. The times are simulated.
32 devices in a mesh: crop: 2 (over y), row: 4 (over z), col: 2 (over x), chan: 2 (over core).
Axes of the slice: x: 2, y: 2, z: 4, core: 2. Of those that a mesh axis runs over, the one named last changes fastest.
Arguments:
- pair_act: bfloat16 [256, 128, 128], P(('crop', 'row'), 'col'), parts along dimension 0, may hold values from -10 to 10
- input_gain: float32 [128], replicated, may hold values from 0.1 to 1.9
- left_proj: bfloat16 [128, 128], replicated, may hold values from -0.5 to 0.5
- left_gate: bfloat16 [128, 128], replicated, may hold values from -0.5 to 0.5
- right_proj: bfloat16 [128, 128], replicated, may hold values from -0.5 to 0.5
- right_gate: bfloat16 [128, 128], replicated, may hold values from -0.5 to 0.5
- output_gain: float32 [128], replicated, may hold values from 0.1 to 1.9
- out_gate: bfloat16 [128, 128], replicated, may hold values from -0.5 to 0.5
- out_proj: bfloat16 [128, 128], replicated, may hold values from -0.5 to 0.5
Outputs:
- update: bfloat16 [256, 128, 128], P(('crop', 'row'), 'col', 'chan'), parts along dimension 0
There are 2 independent parts, one for each index of `crop`. A program takes and returns all parts, laid end to end along the dimension named above; an argument that names none is the same for every part. Nothing has to cross between parts.
All inputs are finite; a program needn't handle non-finite values.
Results may differ from a plain program's by a relative error of at most 0.012.
Values may be sent and summed in bfloat16 or wider, within the bound.
A program may use at most 64 MiB of HBM per device.

v0:
```python
import jax
import jax.numpy as jnp
from jax import lax
from jax.sharding import PartitionSpec as P

epsilon = 1e-05


def spread(x, axis, root):
    mine = lax.axis_index(axis) == root
    return lax.psum(jnp.where(mine, x, jnp.zeros_like(x)), axis)


def normalize(values, scaling):
    average = jnp.mean(values, axis=-1, keepdims=True)
    variance = jnp.mean(values * values, axis=-1, keepdims=True) - average * average
    return (values - average) * lax.rsqrt(variance + epsilon) * scaling


def project(normed, weights):
    flattened = normed.reshape(-1, normed.shape[-1])
    result = jnp.dot(flattened, weights, preferred_element_type=jnp.float32)
    return result.reshape(normed.shape[:-1] + (weights.shape[1],))


def accumulate(column_panel, segment):
    product = lax.dot_general(
        segment, column_panel, (((2,), (2,)), ((0,), (0,))), preferred_element_type=jnp.float32
    )
    return product


def gated_pair(product, hidden):
    left_act = (jax.nn.sigmoid(product[..., hidden : 2 * hidden]) * product[..., :hidden]).astype(
        jnp.bfloat16
    )
    right_act = (
        jax.nn.sigmoid(product[..., 3 * hidden :]) * product[..., 2 * hidden : 3 * hidden]
    ).astype(jnp.bfloat16)
    return (jnp.transpose(left_act, (2, 0, 1)), jnp.transpose(right_act, (2, 0, 1)))


def on_device(
    pair_act,
    input_gain,
    left_proj,
    left_gate,
    right_proj,
    right_gate,
    output_gain,
    out_gate,
    out_proj,
):
    channels = pair_act.shape[2]
    hidden = left_proj.shape[1]
    chan_count = lax.axis_size("chan")
    chan_index = lax.axis_index("chan")
    slab_width = hidden // chan_count
    out_slab = channels // chan_count
    normed = normalize(pair_act.astype(jnp.float32), input_gain).astype(jnp.bfloat16)

    def pick(weights):
        return lax.dynamic_slice_in_dim(weights, chan_index * slab_width, slab_width, 1)

    stacked = jnp.concatenate(
        [pick(left_proj), pick(left_gate), pick(right_proj), pick(right_gate)], 1
    )
    left_major, right_major = gated_pair(project(normed, stacked), slab_width)
    right_rows = lax.all_gather(right_major, "col", axis=2, tiled=True)
    row_ratio = lax.axis_size("row") // lax.axis_size("col")
    col_index = lax.axis_index("col")
    panels = [
        spread(right_rows, "row", col_index * row_ratio + offset_index)
        for offset_index in range(row_ratio)
    ]
    column_panel = jnp.concatenate(panels, 1)
    tri_major = accumulate(column_panel, lax.all_gather(left_major, "col", axis=2, tiled=True))
    triangle = jnp.transpose(tri_major.astype(jnp.bfloat16), (1, 2, 0))
    tri_values = triangle.astype(jnp.float32)
    total_sum, square_sum = lax.psum(
        (jnp.sum(tri_values, axis=-1), jnp.sum(tri_values * tri_values, axis=-1)), "chan"
    )
    average = total_sum[..., None] / hidden
    variance = square_sum[..., None] / hidden - average * average
    scaling = lax.dynamic_slice_in_dim(output_gain, chan_index * slab_width, slab_width, 0)
    tri_norm = ((tri_values - average) * lax.rsqrt(variance + epsilon) * scaling).astype(
        jnp.bfloat16
    )
    slab_rows = lax.dynamic_slice_in_dim(out_proj, chan_index * slab_width, slab_width, 0)
    partial_terms = project(tri_norm, slab_rows)
    mixture = lax.psum_scatter(partial_terms, "chan", scatter_dimension=2, tiled=True)
    gating = jax.nn.sigmoid(
        project(normed, lax.dynamic_slice_in_dim(out_gate, chan_index * out_slab, out_slab, 1))
    )
    return (gating * mixture).astype(jnp.bfloat16)


def solution(mesh):
    placed = (P(("crop", "row"), "col", None), P(), P(), P(), P(), P(), P(), P(), P())
    return jax.shard_map(
        on_device,
        mesh=mesh,
        in_specs=placed,
        out_specs=P(("crop", "row"), "col", "chan"),
        check_vma=False,
    )
```

profile of v0, /device:TPU:1, one launch (start us, length us, event | category | flops | bytes accessed | tf_op | source)
XLA Modules:
  0.0 149.1 jit_solution(179391734126519319)
XLA Ops:
  6.5 0.0 copy-start
  6.5 0.0 all-reduce.4.cloned.1.call-start
  6.5 1.7 %convert_reduce_fusion = (f32[32,64]{1,0:T(8,128)S(1)}, f32[32,64]{1,0:T(8,128)S(1)}) fusion(bf16[32,64,128]{2,1,0:T(8,128)(2,1)} %param.9), kind=kLoop, calls=%fused_computation.3 | loop fusion | flops 1044480 | bytes 540672 | tf_op jit(solution)/shard_map/reduce_sum | solution.py:15
  8.2 0.9 constant_dynamic-slice_fusion
  9.1 0.9 constant_dynamic-slice_fusion.2
  10.0 1.8 %fusion.23 = f32[32,64,256]{2,1,0:T(8,128)S(1)} fusion(bf16[32,64,128]{2,1,0:T(8,128)(2,1)} %param.9, f32[128]{0:T(128)} %param.10, f32[32,64]{1,0:T(8,128)S(1)} %get-tuple-element.20, f32[32,64]{1,0:T(8,128)S(1)} %get-tuple-element.19, bf16[128,64]{1,0:T(8,128)(2,1)S(1)} %get-tuple-element.22, bf16[128,64]{1,0:T(8,128)(2,1)S(1)} %get-tuple-element.23, ...), kind=kOutput, calls=%fused_computation.37 | convolution fusion | flops 135790592 | bytes 2703872 | tf_op jit(solution)/shard_map/dot_general | solution.py:22
  11.8 0.6 fusion.22
  12.4 14.4 %all_gather.7 = bf16[64,32,128]{0,2,1:T(8,128)(2,1)S(1)} all-gather(bf16[64,32,64]{0,2,1:T(8,128)(2,1)S(1)} %get-tuple-element.13), channel_id=1, replica_groups=mesh['crop'=2,'row'=4,'col'=2,'chan'=2] {'col'}, dimensions={2}, use_global_device_ids=true | all-gather | bytes 786432 | tf_op jit(solution)/shard_map/all_gather | solution.py:69
  26.8 1.4 broadcast_select_fusion.1
  28.3 0.0 all-reduce.4.cloned.1.call-update
  28.3 0.0 copy-start.4
  28.3 0.0 reduce-scatter.4.cloned.1.call-start
  28.3 13.0 %all_gather.6 = bf16[64,32,128]{0,2,1:T(8,128)(2,1)S(1)} all-gather(bf16[64,32,64]{0,2,1:T(8,128)(2,1)S(1)} %get-tuple-element.14), channel_id=1, replica_groups=mesh['crop'=2,'row'=4,'col'=2,'chan'=2] {'col'}, dimensions={2}, use_global_device_ids=true | all-gather | bytes 786432 | tf_op jit(solution)/shard_map/all_gather | solution.py:77
  41.3 1.6 %copy.15 = bf16[64,32,128]{2,1,0:T(8,128)(2,1)} copy(bf16[64,32,128]{0,2,1:T(8,128)(2,1)S(1)} %all_gather.6) | data formatting | bytes 1048576 | tf_op jit(solution)/shard_map/all_gather | solution.py:77
  42.9 0.1 dynamic_slice.26
  43.0 74.5 %all-reduce.4.cloned.1.call-done = (bf16[64,32,128]{0,2,1:T(8,128)(2,1)}, bf16[64,32,128]{0,2,1:T(8,128)(2,1)}) async-done(((bf16[64,32,128]{0,2,1:T(8,128)(2,1)}, bf16[64,32,128]{0,2,1:T(8,128)(2,1)}), (bf16[64,32,128]{0,2,1:T(8,128)(2,1)}, bf16[64,32,128]{0,2,1:T(8,128)(2,1)})) %all-reduce.4.cloned.1.call-update) | async-done | bytes 1048592 | tf_op jit(solution)/shard_map/psum | solution.py:11
  117.5 1.9 %pad_maximum_fusion = bf16[64,64,128]{0,2,1:T(8,128)(2,1)S(1)} fusion(bf16[64,32,128]{0,2,1:T(8,128)(2,1)} %get-tuple-element.11, bf16[64,32,128]{0,2,1:T(8,128)(2,1)} %get-tuple-element.12), kind=kLoop, calls=%fused_computation | loop fusion | flops 524288 | bytes 2097152 | tf_op jit(solution)/shard_map/concatenate | solution.py:76
  119.5 1.7 %copy.16 = bf16[64,64,128]{2,1,0:T(8,128)(2,1)S(1)} copy(bf16[64,64,128]{0,2,1:T(8,128)(2,1)S(1)} %pad_maximum_fusion) | data formatting | bytes 2097152 | tf_op jit(solution)/shard_map/concatenate | solution.py:76
  121.2 1.7 %fusion.39 = (f32[32,64]{1,0:T(8,128)S(1)}, f32[32,64]{1,0:T(8,128)S(1)}, f32[32,64,64]{1,0,2:T(8,128)S(1)}) fusion(bf16[64,32,128]{2,1,0:T(8,128)(2,1)} %copy.15, bf16[64,64,128]{2,1,0:T(8,128)(2,1)S(1)} %copy.16), kind=kOutput, calls=%fused_computation.60 | convolution fusion | flops 34205696 | bytes 2113536 | tf_op jit(solution)/shard_map/dot_general | solution.py:27
  122.9 3.9 %all-reduce = (f32[32,64]{1,0:T(8,128)S(1)}, f32[32,64]{1,0:T(8,128)S(1)}) all-reduce(f32[32,64]{1,0:T(8,128)S(1)} %get-tuple-element.6, f32[32,64]{1,0:T(8,128)S(1)} %get-tuple-element.5), channel_id=1, replica_groups=mesh['crop'=2,'row'=4,'col'=2,'chan'=2] {'chan'}, use_global_device_ids=true, to_apply=%region_7.8 | all-reduce | flops 4096 | bytes 32768 | tf_op jit(solution)/shard_map/psum | solution.py:80
  126.8 0.2 multiply_convert_fusion
  127.0 0.4 fusion.19
  127.4 1.8 %copy.18 = f32[32,64,128]{1,0,2:T(8,128)S(1)} copy(f32[32,64,128]{2,1,0:T(8,128)S(1)} %fusion.19) | data formatting | bytes 2097152
  129.3 1.6 %reshape.43 = f32[128,2048]{1,0:T(8,128)} reshape(f32[128,32,64]{2,1,0:T(8,128)S(1)} %bitcast.20) | data formatting | bytes 2097152
  130.9 0.0 reduce-scatter.4.cloned.1.call-update
  130.9 0.0 copy-start.1
  130.9 0.0 copy-start.2
  130.9 0.0 copy-start.3
  131.0 7.5 %reduce-scatter.4.cloned.1.call-done = f32[64,2048]{1,0:T(8,128)} async-done(((f32[128,2048]{1,0:T(8,128)}), f32[64,2048]{1,0:T(8,128)}) %reduce-scatter.4.cloned.1.call-update) | async-done | bytes 524304
  138.5 1.5 reshape.44
  139.9 0.6 copy.19
  140.6 1.7 %fusion.4 = bf16[32,64,64]{2,1,0:T(8,128)(2,1)} fusion(f32[32,64,64]{2,1,0:T(8,128)S(1)} %copy.19, bf16[32,64,128]{2,1,0:T(8,128)(2,1)S(1)} %copy-done.1, f32[128]{0:T(128)S(1)} %copy-done.2, f32[32,64]{1,0:T(8,128)S(1)} %get-tuple-element.20, f32[32,64]{1,0:T(8,128)S(1)} %get-tuple-element.19, bf16[128,128]{1,0:T(8,128)(2,1)S(1)} %copy-done.3, s32[]{:T(128)S(6)} %select_n.23), kind=kOutput, calls=%fused_computation.9 | convolution fusion | flops 35520512 | bytes 1360388 | tf_op jit(solution)/shard_map/dot_general | solution.py:22
  (7 shorter events, 0.0 us)
Async XLA Ops:
  6.5 120.5 %copy-start = (bf16[128,128]{1,0:T(8,128)(2,1)S(1)}, bf16[128,128]{1,0:T(8,128)(2,1)}, u32[]{:S(2)}) copy-start(bf16[128,128]{1,0:T(8,128)(2,1)} %param.17) | copy-start | bytes 98308
  6.5 111.0 %all-reduce.4.cloned.1.call-start = ((), (), s32[]{:S(2)}) async-start(), calls=%async_computation.2 | async-start | bytes 4194304 | tf_op jit(solution)/shard_map/psum | solution.py:11
  28.3 14.7 %copy-start.4 = (f32[128]{0:T(128)S(1)}, f32[128]{0:T(128)}, u32[]{:S(2)}) copy-start(f32[128]{0:T(128)} %param.15) | copy-start | bytes 1540
  28.3 110.2 %reduce-scatter.4.cloned.1.call-start = ((), (), s32[]{:S(2)}) async-start(), calls=%async_computation.1 | async-start | bytes 1572864
  130.9 9.6 %copy-start.1 = (bf16[32,64,128]{2,1,0:T(8,128)(2,1)S(1)}, bf16[32,64,128]{2,1,0:T(8,128)(2,1)}, u32[]{:S(2)}) copy-start(bf16[32,64,128]{2,1,0:T(8,128)(2,1)} %param.9) | copy-start | bytes 1572868
  130.9 9.6 %copy-start.2 = (f32[128]{0:T(128)S(1)}, f32[128]{0:T(128)}, u32[]{:S(2)}) copy-start(f32[128]{0:T(128)} %param.10) | copy-start | bytes 1540
  130.9 9.6 %copy-start.3 = (bf16[128,128]{1,0:T(8,128)(2,1)S(1)}, bf16[128,128]{1,0:T(8,128)(2,1)}, u32[]{:S(2)}) copy-start(bf16[128,128]{1,0:T(8,128)(2,1)} %param.16) | copy-start | bytes 98308
Sparse Core Ops, SparseCore 0:
  28.4 89.1 all-reduce.3
  131.0 7.3 reduce-scatter.3
where the time goes:
time: 150 us; the launch traced here: 149 us
  waiting for transfers between devices  82.1 us (55%)
  blocking collectives  31.3 us (21%)
  between operations  13.6 us (9%)
  local copies, waits for them, and re-layouts  10.7 us (7%)
  other arithmetic  5.87 us (4%)
  matrix products  5.64 us (4%)
    psum x1, waiting for transfers between devices, spread(): return lax.psum(jnp.where(mine, x, jnp.zeros_like(x)), axis)  74.5 us
    all_gather x1, blocking collectives, on_device(): right_rows = lax.all_gather(right_major, 'col', axis=2, tiled=True)  14.4 us
    all_gather x1, blocking collectives, on_device(): lax.all_gather(left_major, 'col', axis=2, tiled=True)  13 us
    unnamed x3, waiting for transfers between devices  7.53 us
    unnamed x14, local copies, waits for them, and re-layouts  5.57 us
    dot_general x3, matrix products, project(): result = jnp.dot(flattened, weights, preferred_element_type=jnp.float32)  3.93 us
    psum x1, blocking collectives, on_device(): lax.psum((jnp.sum(tri_values, axis=-1), jnp.sum(tri_values * tri_values,...  3.91 us
  transfers between devices with their start and end apart: 2, of which 2 were waited for; matrix products, arithmetic and copies ran while one was open for 1% of the time, Pallas kernels for 0%

commit v1 on v0

v1 whole, which is shorter than its diff:
```python
import functools

import jax
import jax.numpy as jnp
from jax import lax
from jax.experimental import pallas as pl
from jax.experimental.pallas import tpu as pltpu
from jax.sharding import PartitionSpec as P

epsilon = 1e-05
MESH = pl.DeviceIdType.MESH
F32 = jnp.float32
BF16 = jnp.bfloat16
CHUNKS = 4
STEP_GROUPS = 4


def nt_dot(a, b):
    return lax.dot_general(a, b, (((1,), (1,)), ((), ())), preferred_element_type=F32)


def kernel(
    n_row,
    n_col,
    pair_ref,
    in_gain_ref,
    lp_ref,
    lg_ref,
    rp_ref,
    rg_ref,
    out_gain_ref,
    og_ref,
    op_ref,
    out_ref,
    wr,
    wl,
    wo,
    zn,
    flat,
    gate,
    left,
    right,
    keep,
    x_out,
    x_in,
    tri,
    flat_tri,
    z_send,
    z_recv,
    x_send,
    x_recv,
    s_send,
    s_recv,
):
    rows, width, channels = pair_ref.shape
    half = rows // 2
    hidden = lp_ref.shape[1]
    slab = hidden // 2
    pairs = slab // 2
    ratio = n_row // n_col
    per = pairs // CHUNKS
    row = lax.axis_index("row")
    col = lax.axis_index("col")
    chan = lax.axis_index("chan")

    def slot(block):
        return lax.rem(block - ratio * col + n_row, n_row)

    barrier = pltpu.get_barrier_semaphore()

    @pl.when(row + 1 < n_row)
    def _():
        pl.semaphore_signal(barrier, inc=1, device_id={"row": row + 1}, device_id_type=MESH)

    @pl.when(row >= 1)
    def _():
        pl.semaphore_signal(barrier, inc=1, device_id={"row": row - 1}, device_id_type=MESH)

    for d in range(1, n_col):
        pl.semaphore_signal(
            barrier, inc=1, device_id={"col": lax.rem(col + d, n_col)}, device_id_type=MESH
        )
    pl.semaphore_signal(barrier, inc=1, device_id={"chan": 1 - chan}, device_id_type=MESH)

    gain_in = in_gain_ref[...]
    gain_out = out_gain_ref[...]

    def turned(ref, gain):
        w = jnp.transpose(ref[...].astype(F32))
        w = jnp.where(chan == 0, w[:slab], w[slab:])
        return (w * gain).astype(BF16)

    wr[:slab] = turned(rp_ref, gain_in)
    wr[slab:] = turned(rg_ref, gain_in)
    wl[:slab] = turned(lp_ref, gain_in)
    wl[slab : 2 * slab] = turned(lg_ref, gain_in)
    wl[2 * slab :] = turned(og_ref, gain_in)
    wo[...] = turned(op_ref, gain_out)

    low = lax.broadcasted_iota(jnp.int32, (1, 128), 1) < width

    def interleave(a, b):
        first = jnp.where(low, a, pltpu.roll(b, width, 1))
        second = jnp.where(low, pltpu.roll(a, width, 1), b)
        return first, second

    def right_step(t, carry):
        for u in range(STEP_GROUPS):
            g = t * STEP_GROUPS + u
            x = jnp.concatenate([pair_ref[g], pair_ref[g + half]], 0).astype(F32)
            mean = jnp.mean(x, axis=-1, keepdims=True)
            var = jnp.mean(x * x, axis=-1, keepdims=True) - mean * mean
            z = ((x - mean) * lax.rsqrt(var + epsilon)).astype(BF16)
            zn[g] = z
            p = nt_dot(wr[...], z)
            r = jax.nn.sigmoid(p[slab:]) * p[:slab]
            first, second = interleave(r[:pairs], r[pairs:])
            flat[pl.ds(g, pairs, stride=rows), :] = first
            flat[pl.ds(g + half, pairs, stride=rows), :] = second
        return carry

    lax.fori_loop(0, half // STEP_GROUPS, right_step, 0)

    mine = slot(row)

    def z_copy(up, step, q):
        block = row - (step - 1) if up else row + (step - 1)
        there = row + 1 if up else row - 1
        part = right.at[slot(block), pl.ds(q * per, per)]
        lane = 0 if up else 1
        return pltpu.make_async_remote_copy(
            src_ref=part,
            dst_ref=part,
            send_sem=z_send.at[lane, step - 1, q],
            recv_sem=z_recv.at[lane, step - 1, q],
            device_id={"row": there},
            device_id_type=MESH,
        )

    def z_land(up, step, q):
        block = row - step if up else row + step
        part = right.at[slot(block), pl.ds(q * per, per)]
        lane = 0 if up else 1
        return pltpu.make_async_remote_copy(
            src_ref=part,
            dst_ref=part,
            send_sem=z_send.at[lane, step - 1, q],
            recv_sem=z_recv.at[lane, step - 1, q],
            device_id={"row": row},
            device_id_type=MESH,
        )

    def sends(up, step):
        if up:
            return jnp.logical_and(row - (step - 1) >= 0, row + 1 < n_row)
        return jnp.logical_and(row + (step - 1) < n_row, row >= 1)

    def lands(up, step):
        return row - step >= 0 if up else row + step < n_row

    def start_send(step, q):
        for up in (True, False):

            @pl.when(sends(up, step))
            def _():
                z_copy(up, step, q).start()

    def wait_land(step, q):
        for up in (True, False):

            @pl.when(lands(up, step))
            def _():
                z_land(up, step, q).wait_recv()

    middle = jnp.where(row >= 1, 1, 0) + jnp.where(row + 1 < n_row, 1, 0)
    pl.semaphore_wait(barrier, middle + n_col)

    for q in range(CHUNKS):
        span = flat[pl.ds(q * per * rows, per * rows), :].astype(BF16)
        right[mine, pl.ds(q * per, per)] = span.reshape(per, rows, 128)
        start_send(1, q)

    def left_step(t, carry):
        for u in range(STEP_GROUPS):
            g = t * STEP_GROUPS + u
            p = nt_dot(wl[...], zn[g])
            r = jax.nn.sigmoid(p[slab : 2 * slab]) * p[:slab]
            gate[g] = jax.nn.sigmoid(p[2 * slab :])
            first, second = interleave(r[:pairs], r[pairs:])
            flat[pl.ds(g, pairs, stride=rows), :] = first
            flat[pl.ds(g + half, pairs, stride=rows), :] = second
        return carry

    lax.fori_loop(0, half // STEP_GROUPS, left_step, 0)

    def left_mask(t, carry):
        for u in range(per):
            c = t * per + u
            f = flat[pl.ds(pl.multiple_of(c * rows, rows), rows), :]
            first = jnp.where(low, f, 0.0)
            second = jnp.where(low, 0.0, f)
            left[c] = jnp.concatenate(
                [first[:half], second[:half], first[half:], second[half:]], 0
            ).astype(BF16)
        return carry

    for step in range(1, n_row):
        for q in range(CHUNKS):
            if step == 1 and q == 0:
                lax.fori_loop(0, pairs // per, left_mask, 0)
            wait_land(step, q)
            if step + 1 < n_row:
                start_send(step + 1, q)
                continue
            contract(
                q, per, rows, n_row, n_col, col, left, right, keep, x_out, x_in,
                x_send, x_recv, interleave,
            )
            if q >= 1:
                combine(q - 1, per, n_col, col, chan, keep, x_out, x_in, tri, x_send, x_recv, s_send, s_recv)
    combine(CHUNKS - 1, per, n_col, col, chan, keep, x_out, x_in, tri, x_send, x_recv, s_send, s_recv)

    for q in range(CHUNKS):
        s_copy(1 - chan, q, per, chan, tri, s_send, s_recv).wait_recv()

    def stat_step(t, carry):
        total, square = carry
        for u in range(per):
            c = t * per + u
            for h in range(2):
                v = tri[h, c].astype(F32)
                a, b = v[:half], v[half:]
                total = total + (a + b)
                square = square + (a * a + b * b)
        return total, square

    zero = jnp.zeros((half, 128), F32)
    total, square = lax.fori_loop(0, pairs // per, stat_step, (zero, zero))
    mean = total * (1.0 / hidden)
    var = square * (1.0 / hidden) - mean * mean
    scale = lax.rsqrt(var + epsilon)

    def norm_step(t, carry):
        for u in range(per):
            c = t * per + u
            for h in range(2):
                v = tri[h, c].astype(F32)
                for k in range(2):
                    at = pl.multiple_of(((h * 2 + k) * pairs + c) * half, half)
                    flat_tri[pl.ds(at, half), :] = (v[k * half : (k + 1) * half] - mean) * scale
        return carry

    lax.fori_loop(0, pairs // per, norm_step, 0)

    def out_step(t, carry):
        for u in range(STEP_GROUPS):
            g = t * STEP_GROUPS + u
            v = flat_tri[pl.ds(g, hidden, stride=half), :].astype(BF16)
            y = jnp.dot(wo[...], v, preferred_element_type=F32) * gate[g]
            y = jnp.transpose(y).astype(BF16)
            out_ref[g] = y[:width]
            out_ref[g + half] = y[width:]
        return carry

    lax.fori_loop(0, half // STEP_GROUPS, out_step, 0)

    for step in range(1, n_row):
        for q in range(CHUNKS):
            for up in (True, False):

                @pl.when(sends(up, step))
                def _():
                    z_copy(up, step, q).wait_send()

    for q in range(CHUNKS):
        for d in range(1, n_col):
            x_copy(d, q, per, n_col, col, x_out, x_in, x_send, x_recv).wait_send()
        s_copy(chan, q, per, chan, tri, s_send, s_recv).wait_send()


def x_copy(d, q, per, n_col, col, x_out, x_in, x_send, x_recv):
    return pltpu.make_async_remote_copy(
        src_ref=x_out.at[d - 1, pl.ds(q * per, per)],
        dst_ref=x_in.at[d - 1, pl.ds(q * per, per)],
        send_sem=x_send.at[d - 1, q],
        recv_sem=x_recv.at[d - 1, q],
        device_id={"col": lax.rem(col + d, n_col)},
        device_id_type=MESH,
    )


def s_copy(which, q, per, chan, tri, s_send, s_recv):
    part = tri.at[which, pl.ds(q * per, per)]
    return pltpu.make_async_remote_copy(
        src_ref=part,
        dst_ref=part,
        send_sem=s_send.at[q],
        recv_sem=s_recv.at[q],
        device_id={"chan": 1 - chan},
        device_id_type=MESH,
    )


def contract(
    q, per, rows, n_row, n_col, col, left, right, keep, x_out, x_in, x_send, x_recv, interleave
):
    for u in range(per):
        c = q * per + u
        a = left[c]
        for m in range(n_col // 2):
            blocks = n_row // (n_col // 2)
            b = jnp.concatenate([right[m * blocks + s, c] for s in range(blocks)], 0)
            t = nt_dot(a, b)
            even, odd = interleave(t[:rows], t[rows:])
            if m == 0:
                keep[c] = even
            else:
                x_out[2 * m - 1, c] = even.astype(BF16)
            x_out[2 * m, c] = odd.astype(BF16)
    for d in range(1, n_col):
        x_copy(d, q, per, n_col, col, x_out, x_in, x_send, x_recv).start()


def combine(
    q, per, n_col, col, chan, keep, x_out, x_in, tri, x_send, x_recv, s_send, s_recv
):
    for d in range(1, n_col):
        x_copy(d, q, per, n_col, col, x_out, x_in, x_send, x_recv).wait_recv()
    for u in range(per):
        c = q * per + u
        v = keep[c]
        for d in range(1, n_col):
            v = v + x_in[d - 1, c].astype(F32)
        tri[chan, c] = v.astype(BF16)
    s_copy(chan, q, per, chan, tri, s_send, s_recv).start()


def on_device(pair_act, input_gain, lp, lg, rp, rg, output_gain, og, op):
    rows, width, channels = pair_act.shape
    hidden = lp.shape[1]
    slab = hidden // 2
    pairs = slab // 2
    half = rows // 2
    n_row = lax.axis_size("row")
    n_col = lax.axis_size("col")
    vmem = pl.BlockSpec(memory_space=pltpu.VMEM)
    dma = pltpu.SemaphoreType.DMA
    return pl.pallas_call(
        functools.partial(kernel, n_row, n_col),
        out_shape=jax.ShapeDtypeStruct((rows, width, channels // 2), BF16),
        in_specs=[vmem] * 9,
        out_specs=vmem,
        scratch_shapes=[
            pltpu.VMEM((2 * slab, channels), BF16),
            pltpu.VMEM((3 * slab, channels), BF16),
            pltpu.VMEM((channels // 2, hidden), BF16),
            pltpu.VMEM((half, 2 * width, channels), BF16),
            pltpu.VMEM((pairs * rows, 128), F32),
            pltpu.VMEM((half, channels // 2, 128), F32),
            pltpu.VMEM((pairs, 2 * rows, 128), BF16),
            pltpu.VMEM((n_row, pairs, rows, 128), BF16),
            pltpu.VMEM((pairs, rows, 128), F32),
            pltpu.VMEM((n_col - 1, pairs, rows, 128), BF16),
            pltpu.VMEM((n_col - 1, pairs, rows, 128), BF16),
            pltpu.VMEM((2, pairs, rows, 128), BF16),
            pltpu.VMEM((hidden * half, 128), F32),
            dma((2, n_row - 1, CHUNKS)),
            dma((2, n_row - 1, CHUNKS)),
            dma((n_col - 1, CHUNKS)),
            dma((n_col - 1, CHUNKS)),
            dma((CHUNKS,)),
            dma((CHUNKS,)),
        ],
        compiler_params=pltpu.CompilerParams(
            collective_id=0, has_side_effects=True, vmem_limit_bytes=48 * 2**20
        ),
    )(
        pair_act,
        input_gain.reshape(1, channels),
        lp,
        lg,
        rp,
        rg,
        output_gain.reshape(1, hidden),
        og,
        op,
    )


def solution(mesh):
    placed = (P(("crop", "row"), "col", None), P(), P(), P(), P(), P(), P(), P(), P())
    return jax.shard_map(
        on_device,
        mesh=mesh,
        in_specs=placed,
        out_specs=P(("crop", "row"), "col", "chan"),
        check_vma=False,
    )
```

time: 150 us -> 39 us (0.26)
  waiting for transfers between devices: 82.1 us -> 0 us
  Pallas kernels: 0 us -> 31.4 us
  blocking collectives: 31.3 us -> 0 us
  between operations: 13.6 us -> 0.02 us
  other arithmetic: 5.87 us -> 0 us
  matrix products: 5.64 us -> 0 us
  local copies, waits for them, and re-layouts: 10.7 us -> 7.05 us
    psum x1 -> x0, waiting for transfers between devices: 74.5 us -> none  [spread(): return lax.psum(jnp.where(mine, x, jnp.zeros_like(x)), axis)]
    pallas_call x0 -> x1, Pallas kernels: none -> 31.4 us  [on_device(): pl.pallas_call(functools.partial(kernel, n_row, n_col), out_shape=jax.Sha...]
    all_gather x2 -> x0, blocking collectives: 27.3 us -> none  [the longest x1 14.4 us: on_device(): right_rows = lax.all_gather(right_major, 'col', axis=2, tiled=True)]
    unnamed x3 -> x0, waiting for transfers between devices: 7.53 us -> none
    dot_general x4 -> x0, matrix products: 5.64 us -> none  [the longest x3 3.93 us: project(): result = jnp.dot(flattened, weights, preferred_element_type=jnp.float32)]
    psum x1 -> x0, blocking collectives: 3.91 us -> none  [on_device(): lax.psum((jnp.sum(tri_values, axis=-1), jnp.sum(tri_values * tri_values,...]
    concatenate x1 -> x0, other arithmetic: 1.95 us -> none  [on_device(): column_panel = jnp.concatenate(panels, 1)]
    dynamic_slice x3 -> x0, local copies, waits for them, and re-layouts: 1.81 us -> none  [the longest x2 1.74 us: pick(): lax.dynamic_slice_in_dim(weights, chan_index * slab_width, slab_width, 1)]
  transfers between devices with their start and end apart: 2 -> 0, of which waited for: 2 -> 0; matrix products, arithmetic and copies ran while one was open for 1% -> 0% of each run, Pallas kernels for 0% -> 0%
where the time goes in v1:
time: 39 us; the launch traced here: 38.4 us
  Pallas kernels  31.4 us (81%)
  local copies, waits for them, and re-layouts  7.05 us (18%)
    pallas_call x1, Pallas kernels, on_device(): pl.pallas_call(functools.partial(kernel, n_row, n_col), out_shape=jax.Sha...  31.4 us
    unnamed x19, local copies, waits for them, and re-layouts  7.05 us

profile of v1, /device:TPU:1, one launch (start us, length us, event | category | flops | bytes accessed | tf_op | source)
XLA Modules:
  0.0 38.4 jit_solution(11487358673351894681)
XLA Ops:
  0.0 0.0 copy-start.7
  0.0 0.0 copy-start.8
  0.0 0.7 %copy-done.7 = f32[128]{0:T(128)S(1)} copy-done((f32[128]{0:T(128)S(1)}, f32[128]{0:T(128)}, u32[]{:S(2)}) %copy-start.7) | copy-done | bytes 536
  0.7 0.0 copy-done.8
  0.7 0.0 copy-start
  0.7 1.0 %copy-done = bf16[32,64,128]{2,1,0:T(8,128)(2,1)S(1)} copy-done((bf16[32,64,128]{2,1,0:T(8,128)(2,1)S(1)}, bf16[32,64,128]{2,1,0:T(8,128)(2,1)}, u32[]{:S(2)}) %copy-start) | copy-done | bytes 524312
  1.7 0.0 copy-start.1
  1.7 0.8 %copy-done.1 = bf16[128,128]{1,0:T(8,128)(2,1)S(1)} copy-done((bf16[128,128]{1,0:T(8,128)(2,1)S(1)}, bf16[128,128]{1,0:T(8,128)(2,1)}, u32[]{:S(2)}) %copy-start.1) | copy-done | bytes 32792
  2.5 0.0 copy-start.2
  2.5 0.8 %copy-done.2 = bf16[128,128]{1,0:T(8,128)(2,1)S(1)} copy-done((bf16[128,128]{1,0:T(8,128)(2,1)S(1)}, bf16[128,128]{1,0:T(8,128)(2,1)}, u32[]{:S(2)}) %copy-start.2) | copy-done | bytes 32792
  3.2 0.0 copy-start.3
  3.2 0.8 %copy-done.3 = bf16[128,128]{1,0:T(8,128)(2,1)S(1)} copy-done((bf16[128,128]{1,0:T(8,128)(2,1)S(1)}, bf16[128,128]{1,0:T(8,128)(2,1)}, u32[]{:S(2)}) %copy-start.3) | copy-done | bytes 32792
  4.0 0.0 copy-start.4
  4.0 0.8 %copy-done.4 = bf16[128,128]{1,0:T(8,128)(2,1)S(1)} copy-done((bf16[128,128]{1,0:T(8,128)(2,1)S(1)}, bf16[128,128]{1,0:T(8,128)(2,1)}, u32[]{:S(2)}) %copy-start.4) | copy-done | bytes 32792
  4.7 0.0 copy-start.5
  4.8 0.8 %copy-done.5 = bf16[128,128]{1,0:T(8,128)(2,1)S(1)} copy-done((bf16[128,128]{1,0:T(8,128)(2,1)S(1)}, bf16[128,128]{1,0:T(8,128)(2,1)}, u32[]{:S(2)}) %copy-start.5) | copy-done | bytes 32792
  5.5 0.0 copy-start.6
  5.5 0.8 %copy-done.6 = bf16[128,128]{1,0:T(8,128)(2,1)S(1)} copy-done((bf16[128,128]{1,0:T(8,128)(2,1)S(1)}, bf16[128,128]{1,0:T(8,128)(2,1)}, u32[]{:S(2)}) %copy-start.6) | copy-done | bytes 32792
  6.3 31.4 %shard_map.91 = bf16[32,64,64]{2,1,0:T(8,128)(2,1)S(1)} custom-call(bf16[32,64,128]{2,1,0:T(8,128)(2,1)S(1)} %copy-done, f32[1,128]{1,0:T(1,128)S(1)} %bitcast.2, bf16[128,128]{1,0:T(8,128)(2,1)S(1)} %copy-done.1, bf16[128,128]{1,0:T(8,128)(2,1)S(1)} %copy-done.2, bf16[128,128]{1,0:T(8,128)(2,1)S(1)} %copy-done.3, bf16[128,128]{1,0:T(8,128)(2,1)S(1)} %copy-done.4, ...), custom_call_target="tpu_custom_call" | custom-call | tf_op jit(solution)/shard_map/pallas_call | solution.py:348
  37.7 0.8 %copy.11 = bf16[32,64,64]{2,1,0:T(8,128)(2,1)} copy(bf16[32,64,64]{2,1,0:T(8,128)(2,1)S(1)} %shard_map.91) | data formatting | bytes 524288
Async XLA Ops:
  0.0 0.7 %copy-start.7 = (f32[128]{0:T(128)S(1)}, f32[128]{0:T(128)}, u32[]{:S(2)}) copy-start(f32[128]{0:T(128)} %param.10) | copy-start | bytes 1540
  0.0 0.7 %copy-start.8 = (f32[128]{0:T(128)S(1)}, f32[128]{0:T(128)}, u32[]{:S(2)}) copy-start(f32[128]{0:T(128)} %param.15) | copy-start | bytes 1540
  0.7 1.0 %copy-start = (bf16[32,64,128]{2,1,0:T(8,128)(2,1)S(1)}, bf16[32,64,128]{2,1,0:T(8,128)(2,1)}, u32[]{:S(2)}) copy-start(bf16[32,64,128]{2,1,0:T(8,128)(2,1)} %pair_ref.1) | copy-start | bytes 1572868
  1.7 0.8 %copy-start.1 = (bf16[128,128]{1,0:T(8,128)(2,1)S(1)}, bf16[128,128]{1,0:T(8,128)(2,1)}, u32[]{:S(2)}) copy-start(bf16[128,128]{1,0:T(8,128)(2,1)} %lp_ref.1) | copy-start | bytes 98308
  2.5 0.8 %copy-start.2 = (bf16[128,128]{1,0:T(8,128)(2,1)S(1)}, bf16[128,128]{1,0:T(8,128)(2,1)}, u32[]{:S(2)}) copy-start(bf16[128,128]{1,0:T(8,128)(2,1)} %lg_ref.1) | copy-start | bytes 98308
  3.2 0.8 %copy-start.3 = (bf16[128,128]{1,0:T(8,128)(2,1)S(1)}, bf16[128,128]{1,0:T(8,128)(2,1)}, u32[]{:S(2)}) copy-start(bf16[128,128]{1,0:T(8,128)(2,1)} %rp_ref.1) | copy-start | bytes 98308
  4.0 0.8 %copy-start.4 = (bf16[128,128]{1,0:T(8,128)(2,1)S(1)}, bf16[128,128]{1,0:T(8,128)(2,1)}, u32[]{:S(2)}) copy-start(bf16[128,128]{1,0:T(8,128)(2,1)} %rg_ref.1) | copy-start | bytes 98308
  4.7 0.8 %copy-start.5 = (bf16[128,128]{1,0:T(8,128)(2,1)S(1)}, bf16[128,128]{1,0:T(8,128)(2,1)}, u32[]{:S(2)}) copy-start(bf16[128,128]{1,0:T(8,128)(2,1)} %og_ref.1) | copy-start | bytes 98308
  5.5 0.8 %copy-start.6 = (bf16[128,128]{1,0:T(8,128)(2,1)S(1)}, bf16[128,128]{1,0:T(8,128)(2,1)}, u32[]{:S(2)}) copy-start(bf16[128,128]{1,0:T(8,128)(2,1)} %op_ref.1) | copy-start | bytes 98308

commit v2 on v1

--- a/solution.py
+++ b/solution.py
@@ -22,16 +22,20 @@
 def kernel(
     n_row,
     n_col,
+    pair_hbm,
+    in_gain_hbm,
+    lp_hbm,
+    lg_hbm,
+    rp_hbm,
+    rg_hbm,
+    out_gain_hbm,
+    og_hbm,
+    op_hbm,
+    out_ref,
     pair_ref,
-    in_gain_ref,
-    lp_ref,
-    lg_ref,
-    rp_ref,
-    rg_ref,
-    out_gain_ref,
-    og_ref,
-    op_ref,
-    out_ref,
+    gains,
+    weights,
+    in_sem,
     wr,
     wl,
     wo,
@@ -52,9 +56,9 @@
     s_send,
     s_recv,
 ):
-    rows, width, channels = pair_ref.shape
+    rows, width, channels = pair_hbm.shape
     half = rows // 2
-    hidden = lp_ref.shape[1]
+    hidden = lp_hbm.shape[1]
     slab = hidden // 2
     pairs = slab // 2
     ratio = n_row // n_col
@@ -66,6 +70,25 @@
     def slot(block):
         return lax.rem(block - ratio * col + n_row, n_row)
 
+    fetches = [
+        pltpu.make_async_copy(source, target, in_sem.at[index])
+        for index, (source, target) in enumerate(
+            [
+                (rp_hbm, weights.at[0]),
+                (rg_hbm, weights.at[1]),
+                (in_gain_hbm, gains.at[0]),
+                (pair_hbm, pair_ref),
+                (lp_hbm, weights.at[2]),
+                (lg_hbm, weights.at[3]),
+                (og_hbm, weights.at[4]),
+                (op_hbm, weights.at[5]),
+                (out_gain_hbm, gains.at[1]),
+            ]
+        )
+    ]
+    for fetch in fetches:
+        fetch.start()
+
     barrier = pltpu.get_barrier_semaphore()
 
     @pl.when(row + 1 < n_row)
@@ -82,20 +105,17 @@
         )
     pl.semaphore_signal(barrier, inc=1, device_id={"chan": 1 - chan}, device_id_type=MESH)
 
-    gain_in = in_gain_ref[...]
-    gain_out = out_gain_ref[...]
-
-    def turned(ref, gain):
-        w = jnp.transpose(ref[...].astype(F32))
+    def turned(index, gain):
+        w = jnp.transpose(weights[index].astype(F32))
         w = jnp.where(chan == 0, w[:slab], w[slab:])
         return (w * gain).astype(BF16)
 
-    wr[:slab] = turned(rp_ref, gain_in)
-    wr[slab:] = turned(rg_ref, gain_in)
-    wl[:slab] = turned(lp_ref, gain_in)
-    wl[slab : 2 * slab] = turned(lg_ref, gain_in)
-    wl[2 * slab :] = turned(og_ref, gain_in)
-    wo[...] = turned(op_ref, gain_out)
+    for fetch in fetches[:3]:
+        fetch.wait()
+    gain_in = gains[0]
+    wr[:slab] = turned(0, gain_in)
+    wr[slab:] = turned(1, gain_in)
+    fetches[3].wait()
 
     low = lax.broadcasted_iota(jnp.int32, (1, 128), 1) < width
 
@@ -179,6 +199,13 @@
         span = flat[pl.ds(q * per * rows, per * rows), :].astype(BF16)
         right[mine, pl.ds(q * per, per)] = span.reshape(per, rows, 128)
         start_send(1, q)
+
+    for fetch in fetches[4:]:
+        fetch.wait()
+    wl[:slab] = turned(2, gain_in)
+    wl[slab : 2 * slab] = turned(3, gain_in)
+    wl[2 * slab :] = turned(4, gain_in)
+    wo[...] = turned(5, gains[1])
 
     def left_step(t, carry):
         for u in range(STEP_GROUPS):
@@ -348,9 +375,13 @@
     return pl.pallas_call(
         functools.partial(kernel, n_row, n_col),
         out_shape=jax.ShapeDtypeStruct((rows, width, channels // 2), BF16),
-        in_specs=[vmem] * 9,
+        in_specs=[pl.BlockSpec(memory_space=pltpu.HBM)] * 9,
         out_specs=vmem,
         scratch_shapes=[
+            pltpu.VMEM((rows, width, channels), BF16),
+            pltpu.VMEM((2, 1, 128), F32),
+            pltpu.VMEM((6, channels, hidden), BF16),
+            dma((9,)),
             pltpu.VMEM((2 * slab, channels), BF16),
             pltpu.VMEM((3 * slab, channels), BF16),
             pltpu.VMEM((channels // 2, hidden), BF16),
@@ -372,7 +403,7 @@
             dma((CHUNKS,)),
         ],
         compiler_params=pltpu.CompilerParams(
-            collective_id=0, has_side_effects=True, vmem_limit_bytes=48 * 2**20
+            collective_id=0, has_side_effects=True, vmem_limit_bytes=60 * 2**20
         ),
     )(
         pair_act,

time: 39 us -> 35.3 us (0.905)
  local copies, waits for them, and re-layouts: 7.05 us -> 1.87 us
  Pallas kernels: 31.4 us -> 33.2 us
    unnamed x19 -> x1, local copies, waits for them, and re-layouts: 7.05 us -> 1.87 us
    pallas_call x1, Pallas kernels: 31.4 us -> 33.2 us  [on_device(): pl.pallas_call(functools.partial(kernel, n_row, n_col), out_shape=jax.Sha...]
where the time goes in v2:
time: 35.3 us; the launch traced here: 35.1 us
  Pallas kernels  33.2 us (94%)
  local copies, waits for them, and re-layouts  1.87 us (5%)
    pallas_call x1, Pallas kernels, on_device(): pl.pallas_call(functools.partial(kernel, n_row, n_col), out_shape=jax.Sha...  33.2 us
    unnamed x1, local copies, waits for them, and re-layouts  1.87 us

profile of v2, /device:TPU:1, one launch (start us, length us, event | category | flops | bytes accessed | tf_op | source)
XLA Modules:
  0.0 35.1 jit_solution(7101191633101964730)
XLA Ops:
  0.0 33.2 %shard_map.91 = bf16[32,64,64]{2,1,0:T(8,128)(2,1)} custom-call(bf16[32,64,128]{2,1,0:T(8,128)(2,1)} %pair_hbm.1, f32[1,128]{1,0:T(1,128)} %bitcast.2, bf16[128,128]{1,0:T(8,128)(2,1)} %lp_hbm.1, bf16[128,128]{1,0:T(8,128)(2,1)} %lg_hbm.1, bf16[128,128]{1,0:T(8,128)(2,1)} %rp_hbm.1, bf16[128,128]{1,0:T(8,128)(2,1)} %rg_hbm.1, f32[1,128]{1,0:T(1,128)} %bitcast.3, ...), custom_call_target="tpu_custom_call" | custom-call | tf_op jit(solution)/shard_map/pallas_call | solution.py:375
  33.2 1.9 %copy.11 = bf16[32,64,64]{2,1,0:T(8,128)(2,1)} copy(bf16[32,64,64]{2,1,0:T(8,128)(2,1)} %shard_map.91) | data formatting | bytes 524288

commit v3 on v2

--- a/solution.py
+++ b/solution.py
@@ -49,6 +49,10 @@
     x_in,
     tri,
     flat_tri,
+    left_flat,
+    left_end,
+    far_out,
+    far_in,
     z_send,
     z_recv,
     x_send,
@@ -192,13 +196,66 @@
             def _():
                 z_land(up, step, q).wait_recv()
 
+    line_of_four = n_row == 4 and n_col == 2
+    helper = jnp.logical_or(row == 1, row == 2)
+    end = jnp.logical_or(row == 0, row == 3)
+    peer = row + 1 - 2 * lax.rem(row, 2)
+    far_col = 1 - row // 2
+    far_kept = far_col == col
+
+    def hop(index, q, source, target, there):
+        a, b = index
+        return pltpu.make_async_remote_copy(
+            src_ref=source.at[pl.ds(q * per, per)],
+            dst_ref=target.at[pl.ds(q * per, per)],
+            send_sem=z_send.at[a, b, q],
+            recv_sem=z_recv.at[a, b, q],
+            device_id={"row": there},
+            device_id_type=MESH,
+        )
+
+    def block_hop(index, q, block, there):
+        part = right.at[slot(block)]
+        return hop(index, q, part, part, there)
+
+    def to_peer(q):
+        return block_hop((0, 0), q, row, peer)
+
+    def from_peer(q):
+        return block_hop((0, 0), q, peer, peer)
+
+    def to_middle(q):
+        return block_hop((0, 1), q, row, 3 - row)
+
+    def from_middle(q):
+        return block_hop((0, 1), q, 3 - row, 3 - row)
+
+    def pass_on(q):
+        return block_hop((0, 2), q, peer, 3 - row)
+
+    def passed_on(q):
+        return block_hop((0, 2), q, 3 - peer, 3 - row)
+
+    def left_over(q):
+        return hop((1, 0), q, left_flat, left_end, peer)
+
+    def far_back(q):
+        return hop((1, 1), q, far_out, far_in, peer)
+
     middle = jnp.where(row >= 1, 1, 0) + jnp.where(row + 1 < n_row, 1, 0)
     pl.semaphore_wait(barrier, middle + n_col)
 
     for q in range(CHUNKS):
         span = flat[pl.ds(q * per * rows, per * rows), :].astype(BF16)
         right[mine, pl.ds(q * per, per)] = span.reshape(per, rows, 128)
-        start_send(1, q)
+        if line_of_four:
+            to_peer(q).start()
+
+            @pl.when(helper)
+            def _():
+                to_middle(q).start()
+        else:
+            start_send(1, q)
 
     for fetch in fetches[4:]:
         fetch.wait()
@@ -220,21 +277,94 @@
 
     lax.fori_loop(0, half // STEP_GROUPS, left_step, 0)
 
+    def masked(f):
+        first = jnp.where(low, f, 0.0)
+        second = jnp.where(low, 0.0, f)
+        return jnp.concatenate(
+            [first[:half], second[:half], first[half:], second[half:]], 0
+        ).astype(BF16)
+
     def left_mask(t, carry):
         for u in range(per):
             c = t * per + u
             f = flat[pl.ds(pl.multiple_of(c * rows, rows), rows), :]
-            first = jnp.where(low, f, 0.0)
-            second = jnp.where(low, 0.0, f)
-            left[c] = jnp.concatenate(
-                [first[:half], second[:half], first[half:], second[half:]], 0
-            ).astype(BF16)
+            left[c] = masked(f)
+            left_flat[c] = f.astype(BF16)
         return carry
 
-    for step in range(1, n_row):
+    lax.fori_loop(0, pairs // per, left_mask, 0)
+
+    for q in range(CHUNKS if line_of_four else 0):
+
+        @pl.when(helper)
+        def _():
+            from_peer(q).wait_recv()
+            pass_on(q).start()
+
+        @pl.when(end)
+        def _():
+            to_peer(q).wait_send()
+            left_over(q).start()
+            from_peer(q).wait_recv()
+            near = slot(2 * (row // 2))
+            for u in range(per):
+                c = q * per + u
+                b = jnp.concatenate([right[near, c], right[near + 1, c]], 0)
+                t = nt_dot(left[c], b)
+                t = jnp.concatenate([t[:rows], t[rows:]], 1)
+                keep[c] = t
+                x_out[0, c] = t.astype(BF16)
+
+            @pl.when(far_kept)
+            def _():
+                x_copy(1, q, per, n_col, col, x_out, x_in, x_send, x_recv).start()
+
+    for q in range(CHUNKS if line_of_four else 0):
+
+        @pl.when(helper)
+        def _():
+            from_middle(q).wait_recv()
+            passed_on(q).wait_recv()
+            left_over(q).wait_recv()
+            for u in range(per):
+                c = q * per + u
+                a = masked(left_end[c].astype(F32))
+                far = slot(2 * far_col)
+                b = jnp.concatenate([right[far, c], right[far + 1, c]], 0)
+                t = nt_dot(a, b)
+                far_out[c] = jnp.concatenate([t[:rows], t[rows:]], 1).astype(BF16)
+            far_back(q).start()
+            contract(
+                q, per, rows, n_row, n_col, col, left, right, keep, x_out, x_in,
+                x_send, x_recv, interleave,
+            )
+
+        @pl.when(end)
+        def _():
+            far_back(q).wait_recv()
+
+            @pl.when(far_kept)
+            def _():
+                for u in range(per):
+                    c = q * per + u
+                    keep[c] = far_in[c].astype(F32)
+
+            @pl.when(jnp.logical_not(far_kept))
+            def _():
+                pltpu.make_async_remote_copy(
+                    src_ref=far_in.at[pl.ds(q * per, per)],
+                    dst_ref=x_in.at[0, pl.ds(q * per, per)],
+                    send_sem=x_send.at[0, q],
+                    recv_sem=x_recv.at[0, q],
+                    device_id={"col": 1 - col},
+                    device_id_type=MESH,
+                ).start()
+
+        if q >= 1:
+            combine(q - 1, per, n_col, col, chan, keep, x_out, x_in, tri, x_send, x_recv, s_send, s_recv)
+
+    for step in range(1, 1 if line_of_four else n_row):
         for q in range(CHUNKS):
-            if step == 1 and q == 0:
-                lax.fori_loop(0, pairs // per, left_mask, 0)
             wait_land(step, q)
             if step + 1 < n_row:
                 start_send(step + 1, q)
@@ -291,7 +421,20 @@
 
     lax.fori_loop(0, half // STEP_GROUPS, out_step, 0)
 
-    for step in range(1, n_row):
+    for q in range(CHUNKS if line_of_four else 0):
+
+        @pl.when(helper)
+        def _():
+            to_peer(q).wait_send()
+            to_middle(q).wait_send()
+            pass_on(q).wait_send()
+            far_back(q).wait_send()
+
+        @pl.when(end)
+        def _():
+            left_over(q).wait_send()
+
+    for step in range(1, 1 if line_of_four else n_row):
         for q in range(CHUNKS):
             for up in (True, False):
 
@@ -395,6 +538,10 @@
             pltpu.VMEM((n_col - 1, pairs, rows, 128), BF16),
             pltpu.VMEM((2, pairs, rows, 128), BF16),
             pltpu.VMEM((hidden * half, 128), F32),
+            pltpu.VMEM((pairs, rows, 128), BF16),
+            pltpu.VMEM((pairs, rows, 128), BF16),
+            pltpu.VMEM((pairs, rows, 128), BF16),
+            pltpu.VMEM((pairs, rows, 128), BF16),
             dma((2, n_row - 1, CHUNKS)),
             dma((2, n_row - 1, CHUNKS)),
             dma((n_col - 1, CHUNKS)),

time: 35.3 us -> 32.4 us (0.918)
  the two profiles are of different devices: /device:TPU:1 before, /device:TPU:3 now
where the time goes in v3:
time: 32.4 us; the launch traced here: 32.2 us
  Pallas kernels  30.4 us (94%)
  local copies, waits for them, and re-layouts  1.87 us (6%)
    pallas_call x1, Pallas kernels, on_device(): pl.pallas_call(functools.partial(kernel, n_row, n_col), out_shape=jax.Sha...  30.4 us
    unnamed x1, local copies, waits for them, and re-layouts  1.87 us

profile of v3, /device:TPU:3, one launch (start us, length us, event | category | flops | bytes accessed | tf_op | source)
XLA Modules:
  0.0 32.2 jit_solution(12472827659976032366)
XLA Ops:
  0.0 30.4 %shard_map.91 = bf16[32,64,64]{2,1,0:T(8,128)(2,1)} custom-call(bf16[32,64,128]{2,1,0:T(8,128)(2,1)} %pair_hbm.1, f32[1,128]{1,0:T(1,128)} %bitcast.2, bf16[128,128]{1,0:T(8,128)(2,1)} %lp_hbm.1, bf16[128,128]{1,0:T(8,128)(2,1)} %lg_hbm.1, bf16[128,128]{1,0:T(8,128)(2,1)} %rp_hbm.1, bf16[128,128]{1,0:T(8,128)(2,1)} %rg_hbm.1, f32[1,128]{1,0:T(1,128)} %bitcast.3, ...), custom_call_target="tpu_custom_call" | custom-call | tf_op jit(solution)/shard_map/pallas_call | solution.py:518
  30.4 1.9 %copy.11 = bf16[32,64,64]{2,1,0:T(8,128)(2,1)} copy(bf16[32,64,64]{2,1,0:T(8,128)(2,1)} %shard_map.91) | data formatting | bytes 524288

commit v4 on v3

--- a/solution.py
+++ b/solution.py
@@ -12,7 +12,7 @@
 F32 = jnp.float32
 BF16 = jnp.bfloat16
 CHUNKS = 4
-STEP_GROUPS = 4
+STEP_GROUPS = 8
 
 
 def nt_dot(a, b):
@@ -360,8 +360,6 @@
                     device_id_type=MESH,
                 ).start()
 
-        if q >= 1:
-            combine(q - 1, per, n_col, col, chan, keep, x_out, x_in, tri, x_send, x_recv, s_send, s_recv)
 
     for step in range(1, 1 if line_of_four else n_row):
         for q in range(CHUNKS):
@@ -375,7 +373,8 @@
             )
             if q >= 1:
                 combine(q - 1, per, n_col, col, chan, keep, x_out, x_in, tri, x_send, x_recv, s_send, s_recv)
-    combine(CHUNKS - 1, per, n_col, col, chan, keep, x_out, x_in, tri, x_send, x_recv, s_send, s_recv)
+    for q in range(0 if line_of_four else CHUNKS - 1, CHUNKS):
+        combine(q, per, n_col, col, chan, keep, x_out, x_in, tri, x_send, x_recv, s_send, s_recv)
 
     for q in range(CHUNKS):
         s_copy(1 - chan, q, per, chan, tri, s_send, s_recv).wait_recv()

time: 32.4 us -> 29.4 us (0.907)
  Pallas kernels: 30.4 us -> 27.4 us
    pallas_call x1, Pallas kernels: 30.4 us -> 27.4 us  [on_device(): pl.pallas_call(functools.partial(kernel, n_row, n_col), out_shape=jax.Sha...]
where the time goes in v4:
time: 29.4 us; the launch traced here: 29.3 us
  Pallas kernels  27.4 us (93%)
  local copies, waits for them, and re-layouts  1.87 us (6%)
    pallas_call x1, Pallas kernels, on_device(): pl.pallas_call(functools.partial(kernel, n_row, n_col), out_shape=jax.Sha...  27.4 us
    unnamed x1, local copies, waits for them, and re-layouts  1.87 us

profile of v4, /device:TPU:3, one launch (start us, length us, event | category | flops | bytes accessed | tf_op | source)
XLA Modules:
  0.0 29.3 jit_solution(17658574486469729004)
XLA Ops:
  0.0 27.4 %shard_map.91 = bf16[32,64,64]{2,1,0:T(8,128)(2,1)} custom-call(bf16[32,64,128]{2,1,0:T(8,128)(2,1)} %pair_hbm.1, f32[1,128]{1,0:T(1,128)} %bitcast.2, bf16[128,128]{1,0:T(8,128)(2,1)} %lp_hbm.1, bf16[128,128]{1,0:T(8,128)(2,1)} %lg_hbm.1, bf16[128,128]{1,0:T(8,128)(2,1)} %rp_hbm.1, bf16[128,128]{1,0:T(8,128)(2,1)} %rg_hbm.1, f32[1,128]{1,0:T(1,128)} %bitcast.3, ...), custom_call_target="tpu_custom_call" | custom-call | tf_op jit(solution)/shard_map/pallas_call | solution.py:517
  27.4 1.9 %copy.11 = bf16[32,64,64]{2,1,0:T(8,128)(2,1)} copy(bf16[32,64,64]{2,1,0:T(8,128)(2,1)} %shard_map.91) | data formatting | bytes 524288
